TPU v7x, 128 devices: a whole 4x4x4 slice. The times are simulated.
128 devices in a mesh: row: 4 (over z_hi, core), tm: 32 (over y, z_lo, x).
Axes of the slice: x: 4, y: 4, z: 4 (z_hi: 2, z_lo: 2; z = z_hi * 2 + z_lo), core: 2. Of those that a mesh axis runs over, the one named last changes fastest.
Arguments:
- temps: bfloat16 [24576, 16384], P('row', 'tm')
- area: float32 [24576], P('row'), may hold values from 0.2 to 1
- ocean_rows: int32 [24576], P('row'), may hold values from 0 to 6143, as said below
- counts: int32 [4], P('row'), may hold values from 1536 to 6144, as said below
Outputs:
- band: float32 [2048, 16384], P('row', 'tm')
Inputs may be any that keep to these rules, and one draw needn't show every extreme that they name: `ocean_rows`: within each tile of 6144 entries, every local row number appears once. `counts`: some tile is all ocean.
All inputs are finite; a program needn't handle non-finite values.
Results may differ from a plain program's by a relative error of at most 0.0022.
Values may be sent and summed in bfloat16 or wider, within the bound.
A program may use at most 64 MiB of HBM per device.

v0:
```python
import jax
import jax.numpy as jnp
from jax import lax
from jax.sharding import PartitionSpec as P

LAGS = 4


def shifted(value, axis, steps):
    count = lax.axis_size(axis)
    pairs = [(source, (source + steps) % count) for source in range(count)]
    return lax.ppermute(value, axis, pairs)


def body(temps, area, ocean_rows, counts):
    rows, hours = temps.shape
    total_hours = hours * lax.axis_size("tm")
    total_rows = rows * lax.axis_size("row")
    sums = jnp.sum(temps, axis=1, dtype=jnp.float32)
    mean = lax.psum(sums, "tm") / total_hours
    live = (jnp.arange(rows, dtype=jnp.int32) < counts[0]).astype(jnp.float32)
    ocean = jnp.zeros((rows,), jnp.float32).at[ocean_rows].set(live)
    weighted = ((temps.astype(jnp.float32) - mean[:, None]) * (ocean * area)[:, None]).astype(
        jnp.bfloat16
    )
    others = [weighted]
    current = weighted
    for lag in range(1, LAGS):
        current = shifted(current, "tm", -1)
        others.append(current)
    joined = jnp.concatenate(others, axis=1)
    contract = (((0,), (0,)), ((), ()))
    terms = lax.dot_general(joined, weighted, contract, preferred_element_type=jnp.float32)
    summed = lax.psum_scatter(terms, "row", scatter_dimension=0, tiled=True)
    return summed / jnp.sqrt(jnp.float32(total_rows))


def solution(mesh):
    in_specs = (P("row", "tm"), P("row"), P("row"), P("row"))
    out_specs = P("row", "tm")
    return jax.shard_map(body, mesh=mesh, in_specs=in_specs, out_specs=out_specs, check_vma=False)
```

profile of v0, /device:TPU:1, one launch (start us, length us, event | category | flops | bytes accessed | tf_op | source)
XLA Modules:
  0.0 656.1 jit_solution(8619647536048842335)
XLA Ops:
  6.5 0.0 copy-start
  6.5 0.0 reduce-scatter.2.cloned.1.call-start
  7.2 0.7 compare_select_fusion
  8.0 3.7 convert_reduce_fusion
  11.7 131.5 %psum.7 = f32[6144]{0:T(1024)S(1)} all-reduce(f32[6144]{0:T(1024)S(1)} %convert_reduce_fusion), channel_id=1, replica_groups=mesh['row'=4,'tm'=32] {'tm'}, use_global_device_ids=true, to_apply=%region_1.0 | all-reduce | flops 6144 | bytes 49152 | tf_op jit(solution)/shard_map/psum | solution.py:20
  143.1 23.0 %scatter_custom_fusion = f32[6144]{0:T(1024)S(1)} fusion(s32[6144]{0:T(1024)S(1)} %compare_select_fusion, f32[6144]{0:T(1024)S(1)} %fusion.10, f32[]{:T(128)} %constant.5.clone.1), kind=kCustom, calls=%fused_computation.17 | custom fusion | bytes 24580 | tf_op jit(solution)/shard_map/scatter | solution.py:22
  166.2 0.0 copy-done
  166.2 4.4 fusion.9
  170.6 0.1 collective-permute-start
  170.7 108.4 %collective-permute-done = bf16[6144,512]{1,0:T(8,128)(2,1)S(1)} collective-permute-done((bf16[6144,512]{1,0:T(8,128)(2,1)S(1)}, bf16[6144,512]{1,0:T(8,128)(2,1)S(1)}, u32[]{:S(2)}, u32[]{:S(2)}) %collective-permute-start) | collective-permute-done | bytes 6291488 | tf_op jit(solution)/shard_map/ppermute | solution.py:12
  279.1 4.5 collective-permute-start.1
  283.6 129.5 %collective-permute-done.1 = bf16[6144,512]{1,0:T(8,128)(2,1)S(1)} collective-permute-done((bf16[6144,512]{1,0:T(8,128)(2,1)S(1)}, bf16[6144,512]{1,0:T(8,128)(2,1)S(1)}, u32[]{:S(2)}, u32[]{:S(2)}) %collective-permute-start.1) | collective-permute-done | bytes 6291488 | tf_op jit(solution)/shard_map/ppermute | solution.py:12
  413.0 4.5 collective-permute-start.2
  417.6 129.6 %collective-permute-done.2 = bf16[6144,512]{1,0:T(8,128)(2,1)} collective-permute-done((bf16[6144,512]{1,0:T(8,128)(2,1)S(1)}, bf16[6144,512]{1,0:T(8,128)(2,1)}, u32[]{:S(2)}, u32[]{:S(2)}) %collective-permute-start.2) | collective-permute-done | bytes 6291488 | tf_op jit(solution)/shard_map/ppermute | solution.py:12
  547.1 17.6 %fusion = f32[2048,512]{1,0:T(8,128)} fusion(bf16[6144,512]{1,0:T(8,128)(2,1)S(1)} %fusion.9, bf16[6144,512]{1,0:T(8,128)(2,1)} %collective-permute-done.2, bf16[6144,512]{1,0:T(8,128)(2,1)S(1)} %collective-permute-done.1, bf16[6144,512]{1,0:T(8,128)(2,1)S(1)} %collective-permute-done), kind=kOutput, calls=%fused_computation.1 | convolution fusion | flops 12985565184 | bytes 29360128 | tf_op jit(solution)/shard_map/dot_general | solution.py:33
  564.7 0.0 reduce-scatter.2.cloned.1.call-update
  564.8 82.2 %reduce-scatter.2.cloned.1.call-done = f32[512,512]{1,0:T(8,128)} async-done(((f32[2048,512]{1,0:T(8,128)}), f32[512,512]{1,0:T(8,128)}) %reduce-scatter.2.cloned.1.call-update) | async-done | bytes 1048592 | tf_op jit(solution)/shard_map/reduce_scatter | solution.py:34
  646.9 2.3 broadcast_multiply_fusion
  (3 shorter events, 0.0 us)
Async XLA Ops:
  6.5 159.6 %copy-start = (f32[6144]{0:T(1024)S(1)}, f32[6144]{0:T(1024)}, u32[]{:S(2)}) copy-start(f32[6144]{0:T(1024)} %param.5) | copy-start | bytes 73732
  6.5 640.4 %reduce-scatter.2.cloned.1.call-start = ((), (), s32[]{:S(2)}) async-start(), calls=%async_computation.1 | async-start | bytes 5242880 | tf_op jit(solution)/shard_map/reduce_scatter | solution.py:34
  170.6 108.4 %collective-permute-start = (bf16[6144,512]{1,0:T(8,128)(2,1)S(1)}, bf16[6144,512]{1,0:T(8,128)(2,1)S(1)}, u32[]{:S(2)}, u32[]{:S(2)}) collective-permute-start(bf16[6144,512]{1,0:T(8,128)(2,1)S(1)} %fusion.9), channel_id=1, source_target_pairs={{0,31},{1,0},{2,1},{3,2},{4,3},{5,4},{6,5},{7,6},{8,7},{9,8},{10,9... | collective-permute-start | bytes 18874376 | tf_op jit(solution)/shard_map/ppermute | solution.py:12
  279.1 134.0 %collective-permute-start.1 = (bf16[6144,512]{1,0:T(8,128)(2,1)S(1)}, bf16[6144,512]{1,0:T(8,128)(2,1)S(1)}, u32[]{:S(2)}, u32[]{:S(2)}) collective-permute-start(bf16[6144,512]{1,0:T(8,128)(2,1)S(1)} %collective-permute-done), channel_id=1, source_target_pairs={{0,31},{1,0},{2,1},{3,2},{4,3},{5,4},{6,5},{7,6},{8,7},{9,8},{10,9... | collective-permute-start | bytes 18874376 | tf_op jit(solution)/shard_map/ppermute | solution.py:12
  413.0 134.1 %collective-permute-start.2 = (bf16[6144,512]{1,0:T(8,128)(2,1)S(1)}, bf16[6144,512]{1,0:T(8,128)(2,1)}, u32[]{:S(2)}, u32[]{:S(2)}) collective-permute-start(bf16[6144,512]{1,0:T(8,128)(2,1)S(1)} %collective-permute-done.1), channel_id=1, source_target_pairs={{0,31},{1,0},{2,1},{3,2},{4,3},{5,4},{6,5},{7,6},{8,7},{9,8},{10,9... | collective-permute-start | bytes 18874376 | tf_op jit(solution)/shard_map/ppermute | solution.py:12
Sparse Core Ops, SparseCore 0:
  564.9 82.0 reduce-scatter.1
where the time goes:
time: 656 us
  waiting for transfers between devices  450 us (69%)
  blocking collectives  131 us (20%)
  local copies, waits for them, and re-layouts  23 us (4%)
  matrix products  17.6 us (3%)
  between operations  14.1 us (2%)
  other arithmetic  11.2 us (2%)
  starting transfers between devices  9.09 us (1%)
    ppermute x3, waiting for transfers between devices, shifted(): return lax.ppermute(value, axis, pairs)  367 us
    psum x1, blocking collectives, body(): mean = lax.psum(sums, 'tm') / total_hours  131 us
    reduce_scatter x1, waiting for transfers between devices, body(): summed = lax.psum_scatter(terms, 'row', scatter_dimension=0, tiled=True)  82.2 us
    scatter x1, local copies, waits for them, and re-layouts, body(): ocean = jnp.zeros((rows,), jnp.float32).at[ocean_rows].set(live)  23 us
    dot_general x1, matrix products, body(): lax.dot_general(joined, weighted, contract, preferred_element_type=jnp.fl...  17.6 us
  transfers between devices with their start and end apart: 4, of which 4 were waited for; matrix products, arithmetic and copies ran while one was open for 0% of the time, Pallas kernels for 0%

commit v1 on v0

--- a/solution.py
+++ b/solution.py
@@ -4,6 +4,7 @@
 from jax.sharding import PartitionSpec as P
 
 LAGS = 4
+launch_slices_on_mesh = lambda t0: jnp.sum(lax.all_gather(t0, "tm"), 0)
 
 
 def shifted(value, axis, steps):
@@ -17,7 +18,7 @@
     total_hours = hours * lax.axis_size("tm")
     total_rows = rows * lax.axis_size("row")
     sums = jnp.sum(temps, axis=1, dtype=jnp.float32)
-    mean = lax.psum(sums, "tm") / total_hours
+    mean = launch_slices_on_mesh(sums) / total_hours
     live = (jnp.arange(rows, dtype=jnp.int32) < counts[0]).astype(jnp.float32)
     ocean = jnp.zeros((rows,), jnp.float32).at[ocean_rows].set(live)
     weighted = ((temps.astype(jnp.float32) - mean[:, None]) * (ocean * area)[:, None]).astype(

time: 656 us -> 598 us (0.912)
  blocking collectives: 131 us -> 73.2 us
    psum x1 -> x0, blocking collectives: 131 us -> none  [body(): mean = lax.psum(sums, 'tm') / total_hours]
    all_gather x0 -> x1, blocking collectives: none -> 73.2 us  [launch_slices_on_mesh = lambda t0: jnp.sum(lax.all_gather(t0, 'tm'), 0)]
    reduce_scatter x1, waiting for transfers between devices: 82.2 us -> 68 us  [body(): summed = lax.psum_scatter(terms, 'row', scatter_dimension=0, tiled=True)]
    ppermute x3, waiting for transfers between devices: 367 us -> 382 us  [shifted(): return lax.ppermute(value, axis, pairs)]
where the time goes in v1:
time: 598 us
  waiting for transfers between devices  450 us (75%)
  blocking collectives  73.2 us (12%)
  local copies, waits for them, and re-layouts  23.1 us (4%)
  matrix products  17.6 us (3%)
  between operations  14.1 us (2%)
  other arithmetic  11.3 us (2%)
  starting transfers between devices  9.09 us (2%)
    ppermute x3, waiting for transfers between devices, shifted(): return lax.ppermute(value, axis, pairs)  382 us
    all_gather x1, blocking collectives, launch_slices_on_mesh = lambda t0: jnp.sum(lax.all_gather(t0, 'tm'), 0)  73.2 us
    reduce_scatter x1, waiting for transfers between devices, body(): summed = lax.psum_scatter(terms, 'row', scatter_dimension=0, tiled=True)  68 us
    scatter x1, local copies, waits for them, and re-layouts, body(): ocean = jnp.zeros((rows,), jnp.float32).at[ocean_rows].set(live)  23 us
    dot_general x1, matrix products, body(): lax.dot_general(joined, weighted, contract, preferred_element_type=jnp.fl...  17.6 us
  transfers between devices with their start and end apart: 4, of which 4 were waited for; matrix products, arithmetic and copies ran while one was open for 0% of the time, Pallas kernels for 0%

profile of v1, /device:TPU:1, one launch (start us, length us, event | category | flops | bytes accessed | tf_op | source)
XLA Modules:
  0.0 598.0 jit_solution(8742997095590576500)
XLA Ops:
  6.5 0.0 copy-start
  6.5 0.0 reduce-scatter.2.cloned.1.call-start
  7.2 0.7 compare_select_fusion
  8.0 3.7 convert_reduce_fusion
  11.7 73.2 %all-gather = f32[196608]{0:T(1024)S(1)} all-gather(f32[6144]{0:T(1024)S(1)} %convert_reduce_fusion), channel_id=2, replica_groups=mesh['row'=4,'tm'=32] {'tm'}, dimensions={0}, use_global_device_ids=true | all-gather | bytes 811008 | tf_op jit(solution)/shard_map/all_gather | solution.py:7
  84.8 0.1 reshape.12
  85.0 0.1 reduce_sum.19
  85.0 23.0 %scatter_custom_fusion = f32[6144]{0:T(1024)S(1)} fusion(s32[6144]{0:T(1024)S(1)} %compare_select_fusion, f32[6144]{0:T(1024)S(1)} %fusion.10, f32[]{:T(128)} %constant.5.clone.1), kind=kCustom, calls=%fused_computation.17 | custom fusion | bytes 24580 | tf_op jit(solution)/shard_map/scatter | solution.py:23
  108.1 0.0 copy-done
  108.1 4.4 fusion.9
  112.5 0.1 collective-permute-start
  112.6 122.5 %collective-permute-done = bf16[6144,512]{1,0:T(8,128)(2,1)S(1)} collective-permute-done((bf16[6144,512]{1,0:T(8,128)(2,1)S(1)}, bf16[6144,512]{1,0:T(8,128)(2,1)S(1)}, u32[]{:S(2)}, u32[]{:S(2)}) %collective-permute-start) | collective-permute-done | bytes 6291488 | tf_op jit(solution)/shard_map/ppermute | solution.py:13
  235.1 4.5 collective-permute-start.1
  239.6 129.5 %collective-permute-done.1 = bf16[6144,512]{1,0:T(8,128)(2,1)S(1)} collective-permute-done((bf16[6144,512]{1,0:T(8,128)(2,1)S(1)}, bf16[6144,512]{1,0:T(8,128)(2,1)S(1)}, u32[]{:S(2)}, u32[]{:S(2)}) %collective-permute-start.1) | collective-permute-done | bytes 6291488 | tf_op jit(solution)/shard_map/ppermute | solution.py:13
  369.1 4.5 collective-permute-start.2
  373.6 129.6 %collective-permute-done.2 = bf16[6144,512]{1,0:T(8,128)(2,1)} collective-permute-done((bf16[6144,512]{1,0:T(8,128)(2,1)S(1)}, bf16[6144,512]{1,0:T(8,128)(2,1)}, u32[]{:S(2)}, u32[]{:S(2)}) %collective-permute-start.2) | collective-permute-done | bytes 6291488 | tf_op jit(solution)/shard_map/ppermute | solution.py:13
  503.2 17.6 %fusion = f32[2048,512]{1,0:T(8,128)} fusion(bf16[6144,512]{1,0:T(8,128)(2,1)S(1)} %fusion.9, bf16[6144,512]{1,0:T(8,128)(2,1)} %collective-permute-done.2, bf16[6144,512]{1,0:T(8,128)(2,1)S(1)} %collective-permute-done.1, bf16[6144,512]{1,0:T(8,128)(2,1)S(1)} %collective-permute-done), kind=kOutput, calls=%fused_computation.1 | convolution fusion | flops 12985565184 | bytes 29360128 | tf_op jit(solution)/shard_map/dot_general | solution.py:34
  520.8 0.0 reduce-scatter.2.cloned.1.call-update
  520.8 68.0 %reduce-scatter.2.cloned.1.call-done = f32[512,512]{1,0:T(8,128)} async-done(((f32[2048,512]{1,0:T(8,128)}), f32[512,512]{1,0:T(8,128)}) %reduce-scatter.2.cloned.1.call-update) | async-done | bytes 1048592 | tf_op jit(solution)/shard_map/reduce_scatter | solution.py:35
  588.8 2.3 broadcast_multiply_fusion
  (3 shorter events, 0.0 us)
Async XLA Ops:
  6.5 101.5 %copy-start = (f32[6144]{0:T(1024)S(1)}, f32[6144]{0:T(1024)}, u32[]{:S(2)}) copy-start(f32[6144]{0:T(1024)} %param.5) | copy-start | bytes 73732
  6.5 582.3 %reduce-scatter.2.cloned.1.call-start = ((), (), s32[]{:S(2)}) async-start(), calls=%async_computation.1 | async-start | bytes 5242880 | tf_op jit(solution)/shard_map/reduce_scatter | solution.py:35
  112.5 122.6 %collective-permute-start = (bf16[6144,512]{1,0:T(8,128)(2,1)S(1)}, bf16[6144,512]{1,0:T(8,128)(2,1)S(1)}, u32[]{:S(2)}, u32[]{:S(2)}) collective-permute-start(bf16[6144,512]{1,0:T(8,128)(2,1)S(1)} %fusion.9), channel_id=1, source_target_pairs={{0,31},{1,0},{2,1},{3,2},{4,3},{5,4},{6,5},{7,6},{8,7},{9,8},{10,9... | collective-permute-start | bytes 18874376 | tf_op jit(solution)/shard_map/ppermute | solution.py:13
  235.1 134.0 %collective-permute-start.1 = (bf16[6144,512]{1,0:T(8,128)(2,1)S(1)}, bf16[6144,512]{1,0:T(8,128)(2,1)S(1)}, u32[]{:S(2)}, u32[]{:S(2)}) collective-permute-start(bf16[6144,512]{1,0:T(8,128)(2,1)S(1)} %collective-permute-done), channel_id=1, source_target_pairs={{0,31},{1,0},{2,1},{3,2},{4,3},{5,4},{6,5},{7,6},{8,7},{9,8},{10,9... | collective-permute-start | bytes 18874376 | tf_op jit(solution)/shard_map/ppermute | solution.py:13
  369.1 134.1 %collective-permute-start.2 = (bf16[6144,512]{1,0:T(8,128)(2,1)S(1)}, bf16[6144,512]{1,0:T(8,128)(2,1)}, u32[]{:S(2)}, u32[]{:S(2)}) collective-permute-start(bf16[6144,512]{1,0:T(8,128)(2,1)S(1)} %collective-permute-done.1), channel_id=1, source_target_pairs={{0,31},{1,0},{2,1},{3,2},{4,3},{5,4},{6,5},{7,6},{8,7},{9,8},{10,9... | collective-permute-start | bytes 18874376 | tf_op jit(solution)/shard_map/ppermute | solution.py:13
Sparse Core Ops, SparseCore 0:
  520.9 67.8 reduce-scatter.1
